TPU v7x, 128 devices: a whole 4x4x4 slice. The times are simulated.
128 devices in a mesh: row: 8 (over z, x_lo), col: 16 (over y, x_hi, core).
Axes of the slice: x: 4 (x_hi: 2, x_lo: 2; x = x_hi * 2 + x_lo), y: 4, z: 4, core: 2. Of those that a mesh axis runs over, the one named last changes fastest.
Arguments:
- left_factor: float32 [20480, 2048], P('row', 'col'), may hold values from -0.125 to 0.125
- right_factor: float32 [2048, 20480], P('row', 'col'), may hold values from -6 to 6
- pair_gap: float32 [2048], P('col'), may hold values from 0.05 to 2
- mask_left: int32 [160, 16], P('row', 'col'), may hold values 0 or 1
- mask_right: int32 [16, 160], P('row', 'col'), may hold values 0 or 1
Outputs:
- update: float32 [20480, 20480], P('row', 'col')
All inputs are finite; a program needn't handle non-finite values. No bound on the sum of `mask_left` or of `mask_right` on one device may be relied on, other than what follows from the above.
Results may differ from a plain program's by a relative error of at most 0.00008.
Values sent between devices are 32-bit elements; how exact they have to be, the bound alone decides.
A program may use at most 128 MiB of HBM per device.

v0:
```python
import jax
import jax.numpy as jnp
from jax import lax
from jax.sharding import PartitionSpec as P

BLK = 128


def expand(factor, mask):
    rows, cols = factor.shape
    shaped = factor.reshape(rows // BLK, BLK, cols // BLK, BLK)
    shaped = shaped * mask.astype(jnp.float32)[:, None, :, None]
    return shaped.reshape(rows, cols)


def per_device(left_factor, right_factor, pair_gap, mask_left, mask_right):
    weights = jnp.exp(-1.5 * pair_gap)
    scaled_left = expand(left_factor, mask_left) * weights[None, :]
    masked_right = expand(right_factor, mask_right)
    whole_right = lax.all_gather(masked_right, "row", axis=0, tiled=True)
    return jnp.dot(
        lax.all_gather(scaled_left, "col", axis=1, tiled=True),
        whole_right,
        precision=lax.Precision.HIGHEST,
        preferred_element_type=jnp.float32,
    )


def solution(mesh):
    return jax.shard_map(
        per_device,
        mesh=mesh,
        in_specs=(P("row", "col"), P("row", "col"), P("col"), P("row", "col"), P("row", "col")),
        out_specs=P("row", "col"),
        check_vma=False,
    )
```

profile of v0, /device:TPU:1, one launch (start us, length us, event | category | flops | bytes accessed | tf_op | source)
XLA Modules:
  0.0 462.9 jit_solution(2977340970508540947)
XLA Ops:
  6.5 0.0 all-gather.5.cloned.1.call-start
  6.5 0.7 convert_element_type.7
  7.2 0.1 copy.6
  7.3 1.7 copy.7
  9.0 0.4 mul.51
  9.4 1.2 bitcast_multiply_fusion
  10.7 0.0 copy-start.1
  10.7 0.0 copy-start.2
  10.7 0.0 copy-start
  10.7 0.0 all-gather.5.cloned.1.call-update
  10.7 0.0 all-gather.3.cloned.1.call-start
  10.8 0.6 copy-done.1
  11.4 0.0 copy-done.2
  11.4 0.1 broadcast_bitcast_fusion
  11.4 0.6 copy-done
  12.0 1.5 multiply_multiply_fusion
  13.5 0.0 all-gather.3.cloned.1.call-update
  13.5 208.2 %all-gather.5.cloned.1.call-done = f32[2048,1280]{0,1:T(8,128)} async-done(((f32[256,1280]{0,1:T(8,128)}), f32[2048,1280]{0,1:T(8,128)}) %all-gather.5.cloned.1.call-update) | async-done | bytes 10485776 | tf_op jit(solution)/shard_map/all_gather | solution.py:20
  221.7 143.8 %all-gather.3.cloned.1.call-done = f32[2560,2048]{1,0:T(8,128)} async-done(((f32[2560,128]{1,0:T(8,128)}), f32[2560,2048]{1,0:T(8,128)}) %all-gather.3.cloned.1.call-update) | async-done | bytes 20971536 | tf_op jit(solution)/shard_map/all_gather | solution.py:22
  365.5 90.5 %fusion = f32[2560,1280]{1,0:T(8,128)} fusion(f32[2560,2048]{1,0:T(8,128)} %all-gather.3.cloned.1.call-done, f32[2048,1280]{0,1:T(8,128)} %all-gather.5.cloned.1.call-done), kind=kOutput, calls=%fused_computation.5 | convolution fusion | flops 80530636800 | bytes 44564480 | tf_op jit(solution)/shard_map/dot_general | solution.py:21
  (2 shorter events, 0.0 us)
Async XLA Ops:
  6.5 215.2 %all-gather.5.cloned.1.call-start = ((), (), s32[]{:S(2)}) async-start(), calls=%async_computation.1 | async-start | bytes 11796480 | tf_op jit(solution)/shard_map/all_gather | solution.py:20
  10.7 0.7 copy-start.1
  10.7 0.7 copy-start.2
  10.7 1.3 copy-start
  10.7 354.8 %all-gather.3.cloned.1.call-start = ((), (), s32[]{:S(2)}) async-start(), calls=%async_computation | async-start | bytes 22282240 | tf_op jit(solution)/shard_map/all_gather | solution.py:22
Sparse Core Ops, SparseCore 0:
  10.8 210.8 all-gather.4
  224.1 141.3 all-gather.2
where the time goes:
time: 463 us
  waiting for transfers between devices  352 us (76%)
  matrix products  90.5 us (20%)
  between operations  13.4 us (3%)
    all_gather x1, waiting for transfers between devices, per_device(): whole_right = lax.all_gather(masked_right, 'row', axis=0, tiled=True)  208 us
    all_gather x1, waiting for transfers between devices, per_device(): lax.all_gather(scaled_left, 'col', axis=1, tiled=True)  144 us
    dot_general x1, matrix products, per_device(): jnp.dot(lax.all_gather(scaled_left, 'col', axis=1, tiled=True), whole_rig...  90.5 us
  transfers between devices with their start and end apart: 2, of which 2 were waited for; matrix products, arithmetic and copies ran while one was open for 0% of the time, Pallas kernels for 0%

commit v1 on v0

v1 whole, which is shorter than its diff:
```python
import jax
import jax.numpy as jnp
from jax import lax
from jax.experimental import pallas as pl
from jax.experimental.pallas import tpu as pltpu
from jax.sharding import PartitionSpec as P

BLK = 128
C = 10
E = 4
H = 5
S = C + E
M_STEP = 4
PIECES = ((0, 3), (3, 3), (6, 2), (8, 2))
UP = (0, 3)
AHEAD = 1
COUNT = 127
MESH = pl.DeviceIdType.MESH


def expand(factor, mask):
    rows, cols = factor.shape
    shaped = factor.reshape(rows // BLK, BLK, cols // BLK, BLK)
    shaped = shaped * mask.astype(jnp.float32)[:, None, :, None]
    return shaped.reshape(rows, cols)


def dense_path(left_factor, right_factor, pair_gap, mask_left, mask_right):
    weights = jnp.exp(-1.5 * pair_gap)
    scaled_left = expand(left_factor, mask_left) * weights[None, :]
    masked_right = expand(right_factor, mask_right)

    def place(i, whole):
        part = lax.dynamic_slice(masked_right, (i // 10 * BLK, i % 10 * BLK), (BLK, BLK))
        part = lax.all_gather(part, "row", axis=0, tiled=False)[:, None]
        return lax.dynamic_update_slice(whole, part, (0, i // 10, 0, i % 10 * BLK))

    whole_right = lax.fori_loop(0, 20, place, jnp.zeros((8, 2, BLK, 1280), jnp.float32)).reshape(2048, 1280)

    def rows(i, update):
        part = lax.all_gather(lax.dynamic_slice_in_dim(scaled_left, i * 64, 64, axis=0), "col", axis=1, tiled=True)
        product = jnp.dot(part, whole_right, precision=lax.Precision.HIGHEST, preferred_element_type=jnp.float32)
        return lax.dynamic_update_slice_in_dim(update, product, i * 64, axis=0)

    return lax.fori_loop(0, 40, rows, jnp.zeros((2560, 1280), jnp.float32))


def gather_kernel(
    mask_l, mask_r, gap, left, right,
    split_l, split_r, meta_l, meta_r, flag_out,
    all_l, all_r, far_r, lv, rv, next_l, next_r, out_l, out_r, exc_l, exc_r, got_l, got_r,
    tile, tiles, tile2, tiles2,
    local_sem, send_sem, chunk_l, chunk_r, far_sem, exc_sem, tile_sem, tile2_sem,
):
    r, c = lax.axis_index("row"), lax.axis_index("col")
    z, xl = r // 2, lax.rem(r, 2)
    y, xh, core = c // 4, lax.rem(c // 2, 2), lax.rem(c, 2)

    def col_of(dy, flip_x, flip_core=False):
        return (lax.rem(y + dy, 4) * 2 + (1 - xh if flip_x else xh)) * 2 + (1 - core if flip_core else core)

    def row_of(dz, flip_x):
        return lax.rem(z + dz, 4) * 2 + (1 - xl if flip_x else xl)

    partner = {"row": r, "col": col_of(0, False, True)}
    used = []
    numbers = iter(range(SENDS))

    def send(src, dst, recv_sem, device):
        copy = pltpu.make_async_remote_copy(
            src_ref=src, dst_ref=dst, send_sem=send_sem.at[next(numbers)], recv_sem=recv_sem,
            device_id=device, device_id_type=MESH,
        )
        copy.start()
        used.append(copy)

    def arrived(ref, recv_sem):
        pltpu.make_async_remote_copy(
            src_ref=ref, dst_ref=ref, send_sem=send_sem.at[0], recv_sem=recv_sem,
            device_id=partner, device_id_type=MESH,
        ).wait_recv()

    loads = [pltpu.make_async_copy(left, lv, local_sem.at[0])]
    for j in range(10):
        loads.append(pltpu.make_async_copy(
            right.at[:, pl.ds(j * BLK, BLK)], rv.at[pl.ds(j * 2 * BLK, 2 * BLK), :], local_sem.at[1 + j]))
    for load in loads:
        load.start()

    barrier = pltpu.get_barrier_semaphore()
    for d in range(1, 16):
        pl.semaphore_signal(barrier, inc=1, device_id={"row": r, "col": lax.rem(c + d, 16)}, device_id_type=MESH)
    for d in range(1, 8):
        pl.semaphore_signal(barrier, inc=1, device_id={"row": lax.rem(r + d, 8), "col": c}, device_id_type=MESH)

    def positions(mask_at, nxt):
        nxt[21] = jnp.int32(20)
        nxt[20] = jnp.int32(20)
        following = jnp.int32(20)
        count = jnp.int32(0)
        for b in reversed(range(20)):
            stored = mask_at(b) != 0
            following = jnp.where(stored, jnp.int32(b), following)
            nxt[b] = following
            count = count + jnp.where(stored, 1, 0)
        at = nxt[0]
        found = [at]
        for _ in range(S - 1):
            at = nxt[at + 1]
            found.append(at)
        return found, count

    pos_l, n_l = positions(lambda b: mask_l[b], next_l)
    pos_r, n_r = positions(lambda b: mask_r[b % 2, b // 2], next_r)
    weights = jnp.exp(-1.5 * gap[...])

    def own_l(t):
        return lv[pl.ds(jnp.minimum(pos_l[t], 19) * BLK, BLK), :] * weights

    def own_r(t):
        return rv[pl.ds(jnp.minimum(pos_r[t], 19) * BLK, BLK), :]

    for load in loads:
        load.wait()
    def pack(first, last):
        for t in range(first, last):
            out_l[t] = own_l(t)
            out_r[t] = own_r(t)

    NP = len(PIECES)
    ready = sum(1 for at, size in PIECES if at + size <= C - E)
    pieces = [pl.ds(at, size) for at, size in PIECES]
    ends = [at + size for at, size in PIECES]
    pack(0, ends[0])
    pl.semaphore_wait(barrier, 22)

    up_l, down_l, over_l = ({"row": r, "col": col_of(d, f)} for d, f in ((1, False), (3, False), (0, True)))
    up_r, down_r, over_r = ({"row": row_of(d, f), "col": c} for d, f in ((1, False), (3, False), (0, True)))

    def pass_l(chip_col, h, to, src=None):
        part = all_l.at[chip_col, pieces[h]]
        for device in to:
            send(part if src is None else src, part, chunk_l.at[chip_col, h], device)

    def pass_r(at_row, h, to, src=None):
        part = all_r.at[at_row, pieces[h]]
        for device in to:
            send(part if src is None else src, part, chunk_r.at[at_row, h], device)

    def pass_far(at_row, src=None):
        send(all_r.at[at_row, pl.ds(C - E, E)] if src is None else src, far_r.at[at_row], far_sem.at[at_row], partner)

    def split(block, at, slot):
        high = block.astype(jnp.bfloat16)
        at[slot, :, 0:BLK] = high
        at[slot, :, BLK:] = (block - high.astype(jnp.float32)).astype(jnp.bfloat16)

    def split_piece_l(chip_col, h, src):
        mate = chip_col + 1 - 2 * lax.rem(chip_col, 2)
        first, size = PIECES[h]

        def one(t, _):
            split(src[t], split_l, chip_col * S + t)
            return 0

        lax.fori_loop(first, first + size, one, 0)
        if first >= C - E:
            def other(t, _):
                split(src[t], split_l, mate * S + 2 * C - 1 - t)
                return 0

            lax.fori_loop(first, first + size, other, 0)

    def split_piece_r(at_row, h, src):
        first, size = PIECES[h]

        def one(t, _):
            split(src[t], split_r, at_row * S + t)
            return 0

        lax.fori_loop(first, first + size, one, 0)

    def keep_l(chip_col, h):
        split_piece_l(chip_col, h, all_l.at[chip_col])

    def keep_r(at_row, h):
        split_piece_r(at_row, h, all_r.at[at_row])

    def await_l(chip_col, h):
        arrived(all_l.at[chip_col, pieces[h]], chunk_l.at[chip_col, h])

    def await_r(at_row, h):
        arrived(all_r.at[at_row, pieces[h]], chunk_r.at[at_row, h])

    def from_partner(d, flip, h):
        chip_col = col_of(d, flip, True)
        await_l(chip_col, h)
        keep_l(chip_col, h)

    def far_blocks(d, flip):
        at_row = row_of(d, flip)
        arrived(far_r.at[at_row], far_sem.at[at_row])

        def one(q, _):
            split(far_r[at_row, q], split_r, at_row * S + S - 1 - q)
            return 0

        lax.fori_loop(0, E, one, 0)

    crossing = {}

    def own_piece(h):
        if h < AHEAD:
            cross(h)
        pass_l(c, h, (up_l, down_l), out_l.at[pieces[h]])
        pass_r(r, h, (up_r, down_r), out_r.at[pieces[h]])
        pass_l(c, h, (partner,), out_l.at[pieces[h]])

    def cross(h):
        pass_l(c, h, (over_l,), out_l.at[pieces[h]])
        pass_r(r, h, (over_r,), out_r.at[pieces[h]])
        crossing[h] = used[-2:]

    def cross_after(h):
        for copy in crossing[h - AHEAD]:
            copy.wait_send()
        used[:] = [copy for copy in used if all(copy is not done for done in crossing[h - AHEAD])]
        cross(h)

    own_piece(0)
    for q in range(E):
        exc_l[q] = own_l(C + q)
        exc_r[q] = own_r(C + q)
    send(exc_l, got_l, exc_sem.at[0], partner)
    send(exc_r, got_r, exc_sem.at[1], partner)
    for h in range(1, ready):
        pack(ends[h - 1], ends[h])
        own_piece(h)

    row_at = lax.broadcasted_iota(jnp.int32, (8, BLK), 0)
    lane_at = lax.broadcasted_iota(jnp.int32, (8, BLK), 1)
    note = jnp.where(lane_at == COUNT, jnp.where(row_at == 0, n_l, n_r), 20)
    for t in range(S):
        note = jnp.where(lane_at == t, jnp.where(row_at == 0, pos_l[t], pos_r[t]), note)
    tile[...] = note
    tiles[c] = note
    for d in range(1, 16):
        send(tile, tiles.at[c], tile_sem.at[c], {"row": r, "col": lax.rem(c + d, 16)})

    arrived(got_l, exc_sem.at[0])
    arrived(got_r, exc_sem.at[1])
    pack(ends[ready - 1], C - E)
    for t in range(C - E, C):
        out_l[t] = jnp.where(t < n_l, own_l(t), got_l[C - 1 - t])
        out_r[t] = jnp.where(t < n_r, own_r(t), got_r[C - 1 - t])
    for h in range(ready, NP):
        own_piece(h)
    pass_far(r, out_r.at[pl.ds(C - E, E)])
    def keep_own():
        for h in range(NP):
            split_piece_l(c, h, out_l)
            split_piece_r(r, h, out_r)

    def lists_l():
        for d in range(1, 16):
            other = lax.rem(c + d, 16)
            arrived(tiles.at[other], tile_sem.at[other])
        over = jnp.zeros((8, BLK), jnp.int32)
        for pair in range(8):
            one, two = tiles[2 * pair], tiles[2 * pair + 1]
            meta_l[pl.ds(2 * pair, 1), :] = one[0:1]
            meta_l[pl.ds(2 * pair + 1, 1), :] = two[0:1]
            full = jnp.where((one > C + E) | (two > C + E) | (one + two > 2 * C), 1, 0)
            over = jnp.maximum(over, full)
        over = jnp.where(lane_at == COUNT, over, 0)
        over = jnp.maximum(over[0:1], over[1:2])
        note2 = jnp.where(row_at == 0, note[1:2], over)
        tile2[...] = note2
        tiles2[r] = note2
        for d in range(1, 8):
            send(tile2, tiles2.at[r], tile2_sem.at[r], {"row": lax.rem(r + d, 8), "col": c})

    def lists_r():
        for d in range(1, 8):
            other = lax.rem(r + d, 8)
            arrived(tiles2.at[other], tile2_sem.at[other])
        flag = jnp.zeros((1, BLK), jnp.int32)
        for k in range(8):
            got = tiles2[k]
            meta_r[pl.ds(k, 1), :] = got[0:1]
            flag = jnp.maximum(flag, got[1:2])
        flag_out[...] = jnp.broadcast_to(flag, (8, BLK))

    def from_x(h):
        mine_l, mine_r = col_of(0, True), row_of(0, True)
        await_r(mine_r, h)
        pass_r(mine_r, h, (up_r, down_r))
        await_l(mine_l, h)
        pass_l(mine_l, h, (up_l, down_l, partner))
        if h == NP - 1:
            pass_far(mine_r)
        keep_r(mine_r, h)
        keep_l(mine_l, h)

    def from_ring(flip, h):
        for d in (3, 1):
            onward = (h in UP) == (d == 3)
            await_l(col_of(d, flip), h)
            pass_l(col_of(d, flip), h, (((up_l if d == 3 else down_l),) if onward else ()) + (partner,))
            await_r(row_of(d, flip), h)
            pass_r(row_of(d, flip), h, ((up_r if d == 3 else down_r),) if onward else ())
            if h == NP - 1:
                pass_far(row_of(d, flip))
        for d in (3, 1):
            keep_l(col_of(d, flip), h)
            keep_r(row_of(d, flip), h)

    def from_far(flip, h):
        await_l(col_of(2, flip), h)
        pass_l(col_of(2, flip), h, (partner,))
        await_r(row_of(2, flip), h)
        if h == NP - 1:
            pass_far(row_of(2, flip))
        keep_l(col_of(2, flip), h)
        keep_r(row_of(2, flip), h)

    events = [(0.12, keep_own, ()), (0.3, lists_l, ()), (1.1, lists_r, ())]
    for h in range(NP):
        share = ends[h] / C
        if h >= AHEAD:
            events.append((2 * ends[h - AHEAD] / C - 0.02, cross_after, (h,)))
        ring, x, far = share, 2 * share, 1 + share
        ring2, far2 = max(1.5, 2 * share) + share / 2 + 0.2, 3 + share
        events.append((ring, from_ring, (False, h)))
        events.append((x, from_x, (h,)))
        events.append((far, from_far, (False, h)))
        events.append((ring2, from_ring, (True, h)))
        events.append((far2, from_far, (True, h)))
        events.append((0.26 + share / 2, from_partner, (0, False, h)))
        for d in (1, 3):
            events.append((ring + 0.3, from_partner, (d, False, h)))
            events.append((ring2 + 0.3, from_partner, (d, True, h)))
        events.append((x + 0.3, from_partner, (0, True, h)))
        events.append((far + 0.3, from_partner, (2, False, h)))
        events.append((far2 + 0.3, from_partner, (2, True, h)))
    for d in range(4):
        for flip in (False, True):
            events.append(((1 if d == 0 else 2) + 1.1 + flip * 0.9 + 0.3 * d, far_blocks, (d, flip)))
    for _, what, how in sorted(events, key=lambda event: event[0]):
        what(*how)
    for copy in used:
        copy.wait_send()


SENDS = 136


def gather(left_factor, right_factor, pair_gap, mask_left, mask_right):
    smem = pl.BlockSpec(memory_space=pltpu.SMEM)
    vmem = pl.BlockSpec(memory_space=pltpu.VMEM)
    hbm = pl.BlockSpec(memory_space=pl.ANY)
    f32, i32 = jnp.float32, jnp.int32
    dma = pltpu.SemaphoreType.DMA
    return pl.pallas_call(
        gather_kernel,
        out_shape=(
            jax.ShapeDtypeStruct((16 * S + M_STEP, BLK, 2 * BLK), jnp.bfloat16),
            jax.ShapeDtypeStruct((8 * S, BLK, 2 * BLK), jnp.bfloat16),
            jax.ShapeDtypeStruct((16, BLK), i32),
            jax.ShapeDtypeStruct((8, BLK), i32),
            jax.ShapeDtypeStruct((8, BLK), i32),
        ),
        in_specs=[smem, smem, vmem, hbm, hbm],
        out_specs=(vmem,) * 5,
        scratch_shapes=[
            pltpu.VMEM((16, C, BLK, BLK), f32), pltpu.VMEM((8, C, BLK, BLK), f32), pltpu.VMEM((8, E, BLK, BLK), f32),
            pltpu.VMEM((20 * BLK, BLK), f32), pltpu.VMEM((20 * BLK, BLK), f32),
            pltpu.SMEM((22,), i32), pltpu.SMEM((22,), i32),
            pltpu.VMEM((C, BLK, BLK), f32), pltpu.VMEM((C, BLK, BLK), f32),
            pltpu.VMEM((E, BLK, BLK), f32), pltpu.VMEM((E, BLK, BLK), f32),
            pltpu.VMEM((E, BLK, BLK), f32), pltpu.VMEM((E, BLK, BLK), f32),
            pltpu.VMEM((8, BLK), i32), pltpu.VMEM((16, 8, BLK), i32),
            pltpu.VMEM((8, BLK), i32), pltpu.VMEM((8, 8, BLK), i32),
            dma((13,)), dma((SENDS,)), dma((16, len(PIECES))), dma((8, len(PIECES))), dma((8,)), dma((2,)), dma((16,)), dma((8,)),
        ],
        compiler_params=pltpu.CompilerParams(
            collective_id=0, has_side_effects=True, vmem_limit_bytes=30 << 20),
    )(mask_left.reshape(20), mask_right, pair_gap.reshape(1, BLK), left_factor, right_factor)


W = 12
ENTRIES = 16 * 5 * 5 + 2


def product_kernel(meta_l, meta_r, split_l, split_r, update, acc, slot_of, strip_of, left_of, right_of, sem_o):
    def count(meta, at):
        return jnp.minimum(meta[at, COUNT], S)

    def zero(i, _):
        rows = pl.ds(pl.multiple_of(lax.rem(i, 10) * 256, 256), 256)
        acc[i // 10, rows, :] = jnp.zeros((256, BLK), jnp.float32)
        return 0

    lax.fori_loop(0, 100, zero, 0)

    def clear(i, _):
        slot_of[i] = jnp.int32(0)
        strip_of[i] = jnp.int32(10)
        return 0

    lax.fori_loop(0, 17 * W, clear, 0, unroll=6)

    def sort_r(k, total):
        def one(t, ends):
            b = meta_r[k, t]
            odd = lax.rem(b, 2)
            place = (2 * k + odd) * W + jnp.where(odd == 1, ends[1], ends[0])
            slot_of[place] = k * S + t
            strip_of[place] = b // 2
            return ends[0] + 1 - odd, ends[1] + odd

        ends = lax.fori_loop(0, count(meta_r, k), one, (jnp.int32(0), jnp.int32(0)))
        for odd in range(2):
            pair = 2 * k + odd
            steps = (count(meta_l, pair) + M_STEP - 1) // M_STEP

            def across(q, total):
                def down(u, total):
                    left_of[total] = pair * 4 + u
                    right_of[total] = pair * W + 2 * q
                    return total + 1

                return lax.fori_loop(0, steps, down, total)

            total = lax.fori_loop(0, (ends[odd] + 1) // 2, across, total)
        return total

    total = lax.fori_loop(0, 8, sort_r, jnp.int32(0))
    left_of[total] = jnp.int32(0)
    right_of[total] = jnp.int32(16 * W)

    def step(n):
        at_l, at_r = left_of[n], right_of[n]
        k, u = at_l // 4, lax.rem(at_l, 4)
        one, two = split_r[slot_of[at_r]], split_r[slot_of[at_r + 1]]
        highs = jnp.concatenate([one[:, :BLK], two[:, :BLK]], axis=1)
        lows = jnp.concatenate([one[:, BLK:], two[:, BLK:]], axis=1)
        weights = jnp.concatenate([highs, highs, lows], axis=0)
        lhs = split_l[pl.ds(k * S + u * M_STEP, M_STEP)].reshape(M_STEP * BLK, 2 * BLK)
        lhs = jnp.concatenate([lhs, lhs[:, :BLK]], axis=1)
        return k, u, at_r, jnp.dot(lhs, weights, preferred_element_type=jnp.float32)

    def store(k, u, at_r, full):
        for v in range(M_STEP):
            rows = pl.ds(pl.multiple_of(meta_l[k, u * M_STEP + v] * BLK, BLK), BLK)
            for w in range(2):
                acc[strip_of[at_r + w], rows, :] += full[v * BLK:(v + 1) * BLK, w * BLK:(w + 1) * BLK]

    def two_steps(n, _):
        first = step(2 * n)
        second = step(2 * n + 1)
        store(*first)
        store(*second)
        return 0

    lax.fori_loop(0, (total + 1) // 2, two_steps, 0)

    outs = [
        pltpu.make_async_copy(acc.at[j, pl.ds(0, 20 * BLK)], update.at[:, pl.ds(j * BLK, BLK)], sem_o.at[j])
        for j in range(10)
    ]
    for copy in outs:
        copy.start()
    for copy in outs:
        copy.wait()


def product(meta_l, meta_r, split_l, split_r):
    smem = pl.BlockSpec(memory_space=pltpu.SMEM)
    vmem = pl.BlockSpec(memory_space=pltpu.VMEM)
    f32, i32 = jnp.float32, jnp.int32
    return pl.pallas_call(
        product_kernel,
        out_shape=jax.ShapeDtypeStruct((20 * BLK, 10 * BLK), f32),
        in_specs=[smem, smem, vmem, vmem],
        out_specs=pl.BlockSpec(memory_space=pl.ANY),
        scratch_shapes=[
            pltpu.VMEM((11, 21 * BLK, BLK), f32),
            pltpu.SMEM((17 * W,), i32), pltpu.SMEM((17 * W,), i32),
            pltpu.SMEM((ENTRIES,), i32), pltpu.SMEM((ENTRIES,), i32),
            pltpu.SemaphoreType.DMA((10,)),
        ],
        compiler_params=pltpu.CompilerParams(vmem_limit_bytes=24 << 20),
    )(meta_l, meta_r, split_l, split_r)


def per_device(left_factor, right_factor, pair_gap, mask_left, mask_right):
    split_l, split_r, meta_l, meta_r, flag = gather(left_factor, right_factor, pair_gap, mask_left, mask_right)
    return lax.cond(
        flag[0, COUNT] > 0,
        lambda: dense_path(left_factor, right_factor, pair_gap, mask_left, mask_right),
        lambda: product(meta_l, meta_r, split_l, split_r),
    )


def solution(mesh):
    return jax.shard_map(
        per_device,
        mesh=mesh,
        in_specs=(P("row", "col"), P("row", "col"), P("col"), P("row", "col"), P("row", "col")),
        out_specs=P("row", "col"),
        check_vma=False,
    )
```

time: 463 us -> 85.2 us (0.18)
  waiting for transfers between devices: 352 us -> 0 us
  matrix products: 90.5 us -> 0 us
  Pallas kernels: 0 us -> 83.8 us
  between operations: 13.4 us -> 0.66 us
    all_gather x2 -> x0, waiting for transfers between devices: 352 us -> none  [the longest x1 208 us: per_device(): whole_right = lax.all_gather(masked_right, 'row', axis=0, tiled=True)]
    dot_general x1 -> x0, matrix products: 90.5 us -> none  [per_device(): jnp.dot(lax.all_gather(scaled_left, 'col', axis=1, tiled=True), whole_rig...]
    pallas_call x0 -> x2, Pallas kernels: none -> 83.8 us  [the longest x1 61.2 us: gather(): pl.pallas_call(gather_kernel, out_shape=(jax.ShapeDtypeStruct((16 * S + M...]
  transfers between devices with their start and end apart: 2 -> 0, of which waited for: 2 -> 0; matrix products, arithmetic and copies ran while one was open for 0% -> 0% of each run, Pallas kernels for 0% -> 0%
where the time goes in v1:
time: 85.2 us; the launch traced here: 85.1 us
  Pallas kernels  83.8 us (98%)
    pallas_call x1, Pallas kernels, gather(): pl.pallas_call(gather_kernel, out_shape=(jax.ShapeDtypeStruct((16 * S + M...  61.2 us
    pallas_call x1, Pallas kernels, product(): pl.pallas_call(product_kernel, out_shape=jax.ShapeDtypeStruct((20 * BLK,...  22.6 us

profile of v1, /device:TPU:1, one launch (start us, length us, event | category | flops | bytes accessed | tf_op | source)
XLA Modules:
  0.0 85.1 jit_solution(13308284112218081537)
XLA Ops:
  0.0 61.2 %shard_map.57 = (bf16[228,128,256]{2,1,0:T(8,128)(2,1)S(1)}, bf16[112,128,256]{2,1,0:T(8,128)(2,1)S(1)}, s32[16,128]{1,0:T(8,128)S(1)}, s32[8,128]{1,0:T(8,128)S(1)}, s32[8,128]{1,0:T(8,128)S(1)}) custom-call(s32[20]{0:T(128)} %bitcast.26, s32[2,10]{1,0:T(2,128)} %mask_r.1, f32[1,128]{1,0:T(1,128)} %bitcast.27, f32[2560,128]{1,0:T(8,128)} %left.1, ...), custom_call_target="tpu_custom_call" | custom-call | tf_op jit(solution)/shard_map/pallas_call | solution.py:364
  61.2 0.6 slice.3
  62.4 22.6 %conditional.1 = (f32[2560,1280]{1,0:T(8,128)}) conditional(s32[]{:T(128)} %bitcast.6, (s32[16,128]{1,0:T(8,128)S(1)}, s32[8,128]{1,0:T(8,128)S(1)}, bf16[228,128,256]{2,1,0:T(8,128)(2,1)S(1)}, bf16[112,128,256]{2,1,0:T(8,128)(2,1)S(1)}) %tuple.47, (s32[20,1]{0,1:T(1,128)}, f32[2560,128]{1,0:T(8,128)}, f32[128]{0:T(128)}, s32[2,10]{1,0:T(2,128)}, ...), branch_computations={%region_0.0_spmd, %region_1.6_spmd} | conditional | flops 2014249216 | bytes 47962932 | solution.py:499
  62.5 22.6 %branch_0_fun.1 = f32[2560,1280]{1,0:T(8,128)} custom-call(s32[16,128]{1,0:T(8,128)S(1)} %get-tuple-element.185.meta_l, s32[8,128]{1,0:T(8,128)S(1)} %get-tuple-element.186.meta_r, bf16[228,128,256]{2,1,0:T(8,128)(2,1)S(1)} %get-tuple-element.187.split_l, bf16[112,128,256]{2,1,0:T(8,128)(2,1)S(1)} %get-tuple-element.188.split_r), custom_call_target="tpu_custom_call" | custom-call | tf_op jit(solution)/shard_map/cond/branch_0_fun/pallas_call | solution.py:482

commit v2 on v1

--- a/solution.py
+++ b/solution.py
@@ -10,7 +10,7 @@
 E = 4
 H = 5
 S = C + E
-M_STEP = 4
+M_STEP = 7
 PIECES = ((0, 3), (3, 3), (6, 2), (8, 2))
 UP = (0, 3)
 AHEAD = 1
@@ -388,27 +388,26 @@
     )(mask_left.reshape(20), mask_right, pair_gap.reshape(1, BLK), left_factor, right_factor)
 
 
+CUTS = (8, 12, 14, 15, 16)
 W = 12
 ENTRIES = 16 * 5 * 5 + 2
 
 
-def product_kernel(meta_l, meta_r, split_l, split_r, update, acc, slot_of, strip_of, left_of, right_of, sem_o):
+def product_kernel(meta_l, meta_r, split_l, split_r, update, acc, slot_of, strip_of, left_of, right_of, steps_of, last_of, sem_o):
     def count(meta, at):
         return jnp.minimum(meta[at, COUNT], S)
 
     def zero(i, _):
         rows = pl.ds(pl.multiple_of(lax.rem(i, 10) * 256, 256), 256)
         acc[i // 10, rows, :] = jnp.zeros((256, BLK), jnp.float32)
+        for n in (2 * i, 2 * i + 1):
+            slot_of[n] = jnp.int32(0)
+            strip_of[n] = jnp.int32(10)
         return 0
 
-    lax.fori_loop(0, 100, zero, 0)
-
-    def clear(i, _):
-        slot_of[i] = jnp.int32(0)
-        strip_of[i] = jnp.int32(10)
-        return 0
-
-    lax.fori_loop(0, 17 * W, clear, 0, unroll=6)
+    lax.fori_loop(0, 17 * W // 2, zero, 0)
+    for j in range(10):
+        last_of[j] = jnp.int32(-1)
 
     def sort_r(k, total):
         def one(t, ends):
@@ -417,6 +416,7 @@
             place = (2 * k + odd) * W + jnp.where(odd == 1, ends[1], ends[0])
             slot_of[place] = k * S + t
             strip_of[place] = b // 2
+            last_of[b // 2] = 2 * k + odd
             return ends[0] + 1 - odd, ends[1] + odd
 
         ends = lax.fori_loop(0, count(meta_r, k), one, (jnp.int32(0), jnp.int32(0)))
@@ -433,6 +433,7 @@
                 return lax.fori_loop(0, steps, down, total)
 
             total = lax.fori_loop(0, (ends[odd] + 1) // 2, across, total)
+            steps_of[pair] = total
         return total
 
     total = lax.fori_loop(0, 8, sort_r, jnp.int32(0))
@@ -463,14 +464,22 @@
         store(*second)
         return 0
 
-    lax.fori_loop(0, (total + 1) // 2, two_steps, 0)
-
     outs = [
         pltpu.make_async_copy(acc.at[j, pl.ds(0, 20 * BLK)], update.at[:, pl.ds(j * BLK, BLK)], sem_o.at[j])
         for j in range(10)
     ]
-    for copy in outs:
-        copy.start()
+    done, before = jnp.int32(0), -1
+    for pairs in CUTS:
+        now = (steps_of[pairs - 1] + 1) // 2
+        lax.fori_loop(done, now, two_steps, 0)
+        for j in range(10):
+            last = last_of[j]
+
+            @pl.when((last >= before) & (last < pairs))
+            def _():
+                outs[j].start()
+
+        done, before = now, pairs
     for copy in outs:
         copy.wait()
 
@@ -488,6 +497,7 @@
             pltpu.VMEM((11, 21 * BLK, BLK), f32),
             pltpu.SMEM((17 * W,), i32), pltpu.SMEM((17 * W,), i32),
             pltpu.SMEM((ENTRIES,), i32), pltpu.SMEM((ENTRIES,), i32),
+            pltpu.SMEM((16,), i32), pltpu.SMEM((10,), i32),
             pltpu.SemaphoreType.DMA((10,)),
         ],
         compiler_params=pltpu.CompilerParams(vmem_limit_bytes=24 << 20),

time: 85.2 us -> 83.6 us (0.981)
  Pallas kernels: 83.8 us -> 81.9 us
    pallas_call x1, Pallas kernels: 22.6 us -> 20.7 us  [product(): pl.pallas_call(product_kernel, out_shape=jax.ShapeDtypeStruct((20 * BLK,...]
where the time goes in v2:
time: 83.6 us; the launch traced here: 83.5 us
  Pallas kernels  81.9 us (98%)
    pallas_call x1, Pallas kernels, gather(): pl.pallas_call(gather_kernel, out_shape=(jax.ShapeDtypeStruct((16 * S + M...  61.2 us
    pallas_call x1, Pallas kernels, product(): pl.pallas_call(product_kernel, out_shape=jax.ShapeDtypeStruct((20 * BLK,...  20.7 us

profile of v2, /device:TPU:1, one launch (start us, length us, event | category | flops | bytes accessed | tf_op | source)
XLA Modules:
  0.0 83.5 jit_solution(7211629515845168459)
XLA Ops:
  0.0 61.2 %shard_map.57 = (bf16[231,128,256]{2,1,0:T(8,128)(2,1)S(1)}, bf16[112,128,256]{2,1,0:T(8,128)(2,1)S(1)}, s32[16,128]{1,0:T(8,128)S(1)}, s32[8,128]{1,0:T(8,128)S(1)}, s32[8,128]{1,0:T(8,128)S(1)}) custom-call(s32[20]{0:T(128)} %bitcast.26, s32[2,10]{1,0:T(2,128)} %mask_r.1, f32[1,128]{1,0:T(1,128)} %bitcast.27, f32[2560,128]{1,0:T(8,128)} %left.1, ...), custom_call_target="tpu_custom_call" | custom-call | tf_op jit(solution)/shard_map/pallas_call | solution.py:364
  61.2 0.6 slice.3
  62.4 20.9 %conditional.1 = (f32[2560,1280]{1,0:T(8,128)}) conditional(s32[]{:T(128)} %bitcast.6, (s32[16,128]{1,0:T(8,128)S(1)}, s32[8,128]{1,0:T(8,128)S(1)}, bf16[231,128,256]{2,1,0:T(8,128)(2,1)S(1)}, bf16[112,128,256]{2,1,0:T(8,128)(2,1)S(1)}) %tuple.47, (s32[20,1]{0,1:T(1,128)}, f32[2560,128]{1,0:T(8,128)}, f32[128]{0:T(128)}, s32[2,10]{1,0:T(2,128)}, ...), branch_computations={%region_0.0_spmd, %region_1.6_spmd} | conditional | flops 2014249216 | bytes 47962932 | solution.py:509
  62.5 20.7 %branch_0_fun.1 = f32[2560,1280]{1,0:T(8,128)} custom-call(s32[16,128]{1,0:T(8,128)S(1)} %get-tuple-element.185.meta_l, s32[8,128]{1,0:T(8,128)S(1)} %get-tuple-element.186.meta_r, bf16[231,128,256]{2,1,0:T(8,128)(2,1)S(1)} %get-tuple-element.187.split_l, bf16[112,128,256]{2,1,0:T(8,128)(2,1)S(1)} %get-tuple-element.188.split_r), custom_call_target="tpu_custom_call" | custom-call | tf_op jit(solution)/shard_map/cond/branch_0_fun/pallas_call | solution.py:491

commit v3 on v2

--- a/solution.py
+++ b/solution.py
@@ -330,7 +330,7 @@
         if h >= AHEAD:
             events.append((2 * ends[h - AHEAD] / C - 0.02, cross_after, (h,)))
         ring, x, far = share, 2 * share, 1 + share
-        ring2, far2 = max(1.5, 2 * share) + share / 2 + 0.2, 3 + share
+        ring2, far2 = max(1.5, 2 * share) + share / 2 + 0.45, 3 + share
         events.append((ring, from_ring, (False, h)))
         events.append((x, from_x, (h,)))
         events.append((far, from_far, (False, h)))

time: 83.6 us -> 80.2 us (0.959)
  the two profiles are of different devices: /device:TPU:1 before, /device:TPU:105 now
where the time goes in v3:
time: 80.2 us; the launch traced here: 79.1 us
  Pallas kernels  77.5 us (97%)
  between operations  0.82 us (1%)
    pallas_call x1, Pallas kernels, gather(): pl.pallas_call(gather_kernel, out_shape=(jax.ShapeDtypeStruct((16 * S + M...  56.5 us
    pallas_call x1, Pallas kernels, product(): pl.pallas_call(product_kernel, out_shape=jax.ShapeDtypeStruct((20 * BLK,...  21 us

profile of v3, /device:TPU:105, one launch (start us, length us, event | category | flops | bytes accessed | tf_op | source)
XLA Modules:
  0.0 79.1 jit_solution(5408068260850689830)
XLA Ops:
  0.0 56.5 %shard_map.57 = (bf16[231,128,256]{2,1,0:T(8,128)(2,1)S(1)}, bf16[112,128,256]{2,1,0:T(8,128)(2,1)S(1)}, s32[16,128]{1,0:T(8,128)S(1)}, s32[8,128]{1,0:T(8,128)S(1)}, s32[8,128]{1,0:T(8,128)S(1)}) custom-call(s32[20]{0:T(128)} %bitcast.26, s32[2,10]{1,0:T(2,128)} %mask_r.1, f32[1,128]{1,0:T(1,128)} %bitcast.27, f32[2560,128]{1,0:T(8,128)} %left.1, ...), custom_call_target="tpu_custom_call" | custom-call | tf_op jit(solution)/shard_map/pallas_call | solution.py:364
  56.5 0.6 slice.3
  57.7 21.2 %conditional.1 = (f32[2560,1280]{1,0:T(8,128)}) conditional(s32[]{:T(128)} %bitcast.6, (s32[16,128]{1,0:T(8,128)S(1)}, s32[8,128]{1,0:T(8,128)S(1)}, bf16[231,128,256]{2,1,0:T(8,128)(2,1)S(1)}, bf16[112,128,256]{2,1,0:T(8,128)(2,1)S(1)}) %tuple.47, (s32[20,1]{0,1:T(1,128)}, f32[2560,128]{1,0:T(8,128)}, f32[128]{0:T(128)}, s32[2,10]{1,0:T(2,128)}, ...), branch_computations={%region_0.0_spmd, %region_1.6_spmd} | conditional | flops 2014249216 | bytes 47962932 | solution.py:509
  57.7 21.0 %branch_0_fun.1 = f32[2560,1280]{1,0:T(8,128)} custom-call(s32[16,128]{1,0:T(8,128)S(1)} %get-tuple-element.185.meta_l, s32[8,128]{1,0:T(8,128)S(1)} %get-tuple-element.186.meta_r, bf16[231,128,256]{2,1,0:T(8,128)(2,1)S(1)} %get-tuple-element.187.split_l, bf16[112,128,256]{2,1,0:T(8,128)(2,1)S(1)} %get-tuple-element.188.split_r), custom_call_target="tpu_custom_call" | custom-call | tf_op jit(solution)/shard_map/cond/branch_0_fun/pallas_call | solution.py:491
